TPU v7x, 512 devices: a whole 4x4x16 slice. The times are simulated.
512 devices in a mesh: lists: 64 (over z, y), users: 8 (over x, core).
Axes of the slice: x: 4, y: 4, z: 16, core: 2. Of those that a mesh axis runs over, the one named last changes fastest.
Arguments:
- user_vectors: bfloat16 [256, 512], P('lists'), may hold values from -6 to 6
- probe_lists: int32 [256, 32], P('lists'), may hold values from 0 to 63, as said below
- list_items: bfloat16 [64, 4096, 512], P('lists', 'users'), may hold values from -6 to 6
- candidate_ids: int32 [64, 512], P('lists'), may hold values from 0 to 262143, as said below
- history: bfloat16 [64, 1024, 512], P('lists', 'users'), may hold values from -6 to 6
- history_lengths: int32 [64], P('lists'), may hold values from 1 to 1024, as said below
- query_weight: bfloat16 [512, 512], replicated, may hold values from -4 to 4
- key_value_weight: bfloat16 [512, 1024], replicated, may hold values from -4 to 4
- out_weight: bfloat16 [512, 512], replicated, may hold values from -3 to 3
Outputs:
- list_scores: bfloat16 [256, 32, 4096], P('lists', None, 'users')
- ranked: bfloat16 [64, 512, 512], P('lists', 'users')
Inputs may be any that keep to these rules, and one draw needn't show every extreme that they name: `probe_lists`: among the probes of the 4 users of one index of lists, no list occurs more than 6 times, and some list exactly 6 times. `candidate_ids`: item i lies in list i // 4096. Among the candidates of the 1 users of one index of lists, at most 3 lie in the same group of 1 lists (list) and the same group of 512 slots (slot // 512), and some such pair of groups holds exactly 3. `history_lengths`: the first ranked user has 1024 valid events.
All inputs are finite; a program needn't handle non-finite values.
Results may differ from a plain program's by a relative error of at most 0.018.
Values may be sent and summed in bfloat16 or wider, within the bound.
A program may use at most 128 MiB of HBM per device.

v0:
```python
import jax
import jax.numpy as jnp
from jax import lax
from jax.sharding import PartitionSpec as P

HEADS = 8


def merged(value, axis, join):
    pieces = jax.tree.map(lambda part: lax.all_gather(part, axis), value)
    head = jax.tree.map(lambda part: part[0], pieces)
    tail = jax.tree.map(lambda part: part[1:], pieces)
    running, _ = lax.scan(lambda running, share: (join(running, share), None), head, tail)
    return running


def bucket_slots(bucket, keep, buckets, most):
    onehot = (bucket[:, None] == jnp.arange(buckets, dtype=jnp.int32)[None, :]).astype(
        jnp.int32
    ) * keep[:, None]
    before = jnp.cumsum(onehot, axis=0) - onehot
    return bucket * most + jnp.sum(before * onehot, axis=1)


def softmax_combine(first, second):
    top = jnp.maximum(first[0], second[0])
    left = jnp.exp(first[0] - top)
    right = jnp.exp(second[0] - top)
    return (
        top,
        first[1] * left + second[1] * right,
        first[2] * left[..., None] + second[2] * right[..., None],
    )


def shards(
    user_vectors,
    probe_lists,
    list_items,
    candidate_ids,
    history,
    history_lengths,
    query_weight,
    key_value_weight,
    out_weight,
):
    n_lists = lax.axis_size("lists")
    n_users = lax.axis_size("users")
    list_dev, items_loc, width = list_items.shape
    user_dev, probes = probe_lists.shape
    total_lists = list_dev * n_lists
    cap_lists = max(2, 3 * user_dev * probes // total_lists)
    scale = width ** (-0.5)
    flat_probes = probe_lists.reshape(-1)
    all_ones = jnp.ones(flat_probes.shape, jnp.int32)
    probe_slot = bucket_slots(flat_probes, all_ones, total_lists, cap_lists)
    repeated = jnp.repeat(user_vectors, probes, axis=0)
    outgoing = (
        jnp.zeros((total_lists * cap_lists, width), jnp.bfloat16).at[probe_slot].set(repeated)
    )
    outgoing = outgoing.reshape(n_lists, list_dev, cap_lists, width)
    scores = jnp.einsum(
        "skcd,kjd->skcj",
        lax.all_to_all(outgoing, "lists", split_axis=0, concat_axis=0, tiled=True),
        list_items,
        preferred_element_type=jnp.float32,
    )
    scores = (scores * scale).astype(jnp.bfloat16)
    returned = lax.all_to_all(scores, "lists", split_axis=0, concat_axis=0, tiled=True)
    returned = returned.reshape(total_lists * cap_lists, items_loc)
    list_scores = returned[probe_slot].reshape(user_dev, probes, items_loc)
    rank_dev, cands = candidate_ids.shape
    grouped = rank_dev * cands
    items_list = items_loc * n_users
    cap_rows = max(2, 3 * grouped // (n_lists * n_users))
    flat_ids = candidate_ids.reshape(-1)
    list_of = flat_ids // items_list
    slot_of = flat_ids % items_list
    owner_row = list_of // list_dev
    owner_col = slot_of // items_loc
    local_index = list_of % list_dev * items_loc + slot_of % items_loc
    flat_items = list_items.reshape(list_dev * items_loc, width)
    column = lax.axis_index("users")
    keep = (owner_col == column).astype(jnp.int32)
    row_slot = bucket_slots(owner_row, keep, n_lists, cap_rows)
    dump = n_lists * cap_rows
    request = (
        jnp.zeros((dump + 1,), jnp.int32).at[jnp.where(keep == 1, row_slot, dump)].set(local_index)
    )
    request = request[:dump].reshape(n_lists, cap_rows)
    fetched = lax.all_to_all(
        flat_items[lax.all_to_all(request, "lists", split_axis=0, concat_axis=0, tiled=True)],
        "lists",
        split_axis=0,
        concat_axis=0,
        tiled=True,
    )
    fetched = fetched.reshape(dump, width)
    mine = jnp.where(
        keep[:, None] == 1,
        fetched[jnp.minimum(row_slot, dump - 1)].astype(jnp.float32),
        jnp.float32(0.0),
    )
    cand_rows = lax.psum(mine.astype(jnp.bfloat16), "users")
    head_dim = width // HEADS
    hist_dev = history.shape[1]
    queries = (
        jnp.dot(cand_rows, query_weight, preferred_element_type=jnp.float32) * head_dim ** (-0.5)
    ).astype(jnp.bfloat16)
    queries = queries.reshape(rank_dev, cands, HEADS, head_dim)
    pairs = jnp.dot(
        history.reshape(-1, width), key_value_weight, preferred_element_type=jnp.float32
    ).astype(jnp.bfloat16)
    pairs = pairs.reshape(rank_dev, hist_dev, 2, HEADS, head_dim)
    positions = column * hist_dev + jnp.arange(hist_dev, dtype=jnp.int32)
    valid_events = positions[None, :] < history_lengths[:, None]

    def attend(packed):
        user_queries, user_pairs, valid = packed
        scores = jnp.einsum(
            "chd,ehd->che", user_queries, user_pairs[:, 0], preferred_element_type=jnp.float32
        )
        mask = valid[None, None, :]
        scores = jnp.where(mask, scores, jnp.float32(-1e30))
        top = jnp.max(scores, axis=-1)
        exponentials = jnp.where(mask, jnp.exp(scores - top[..., None]), jnp.float32(0.0))
        total = jnp.sum(exponentials, axis=-1)
        probs = exponentials.astype(jnp.bfloat16)
        mixed = jnp.einsum(
            "che,ehd->chd", probs, user_pairs[:, 1], preferred_element_type=jnp.float32
        )
        return (top, total, mixed)

    top, total, mixed = lax.map(attend, (queries, pairs, valid_events))
    own = cands // n_users
    top, total, mixed = merged((top, total, mixed), "users", softmax_combine)
    mixed = lax.dynamic_slice_in_dim(mixed, column * own, own, 1)
    total = lax.dynamic_slice_in_dim(total, column * own, own, 1)
    attended = (mixed / total[..., None]).reshape(rank_dev * own, width).astype(jnp.bfloat16)
    ranked = jnp.dot(attended, out_weight, preferred_element_type=jnp.float32).astype(jnp.bfloat16)
    return (list_scores, ranked.reshape(rank_dev, own, width))


def solution(mesh):
    placed = (
        P("lists", None),
        P("lists", None),
        P("lists", "users", None),
        P("lists", None),
        P("lists", "users", None),
        P("lists"),
        P(),
        P(),
        P(),
    )
    return jax.shard_map(
        shards,
        mesh=mesh,
        in_specs=placed,
        out_specs=(P("lists", None, "users"), P("lists", "users", None)),
        check_vma=False,
    )
```

profile of v0, /device:TPU:1, one launch (start us, length us, event | category | flops | bytes accessed | tf_op | source)
XLA Modules:
  0.0 320.3 jit_solution(9531444717493961826)
XLA Ops:
  13.1 2.4 scatter_custom_fusion.1
  15.7 32.5 %all_to_all.27 = s32[64,1,3]{2,1,0:T(1,128)S(1)} all-to-all(s32[64,1,3]{2,1,0:T(1,128)S(1)} %bitcast.151), channel_id=1, replica_groups=mesh['lists'=64,'users'=8] {'lists'}, dimensions={0} | all-to-all | bytes 1536 | tf_op jit(solution)/shard_map/all_to_all | solution.py:92
  50.2 4.6 %all-to-all-start.3 = ((bf16[64,3,512]{2,1,0:T(4,128)(2,1)}), bf16[64,3,512]{2,1,0:T(4,128)(2,1)S(1)}, u32[]{:S(2)}, u32[]{:S(2)}) async-start(bf16[64,3,512]{2,1,0:T(4,128)(2,1)} %reshape.422), calls=%async_computation.3 | async-start | bytes 524288 | tf_op jit(solution)/shard_map/all_to_all | solution.py:91
  55.6 17.7 %all-to-all-done.3 = bf16[64,3,512]{2,1,0:T(4,128)(2,1)S(1)} async-done(((bf16[64,3,512]{2,1,0:T(4,128)(2,1)}), bf16[64,3,512]{2,1,0:T(4,128)(2,1)S(1)}, u32[]{:S(2)}, u32[]{:S(2)}) %all-to-all-start.3) | async-done | bytes 196640 | tf_op jit(solution)/shard_map/all_to_all | solution.py:91
  73.4 2.0 gather_fusion.2
  77.0 69.2 %all-reduce.2.cloned.1.call-done = bf16[512,512]{1,0:T(8,128)(2,1)} async-done(((bf16[512,512]{1,0:T(8,128)(2,1)}), bf16[512,512]{1,0:T(8,128)(2,1)}) %all-reduce.2.cloned.1.call-update) | async-done | bytes 524304 | tf_op jit(solution)/shard_map/psum | solution.py:104
  148.3 1.7 convolution_bitcast_fusion
  154.3 43.1 %all_to_all.28 = bf16[64,1,6,512]{3,2,1,0:T(8,128)(2,1)S(1)} all-to-all(bf16[64,1,6,512]{3,2,1,0:T(8,128)(2,1)} %bitcast.145), channel_id=1, replica_groups=mesh['lists'=64,'users'=8] {'lists'}, dimensions={0} | all-to-all | bytes 786432 | tf_op jit(solution)/shard_map/all_to_all | solution.py:64
  199.9 9.1 %all-to-all-start.1 = ((bf16[64,1,6,512]{3,2,1,0:T(8,128)(2,1)}), bf16[64,1,6,512]{3,2,1,0:T(8,128)(2,1)}, u32[]{:S(2)}, u32[]{:S(2)}) async-start(bf16[64,1,6,512]{3,2,1,0:T(8,128)(2,1)} %copy.32), calls=%async_computation.1 | async-start | bytes 1048576 | tf_op jit(solution)/shard_map/all_to_all | solution.py:69
  209.0 15.7 %all-gather = f32[4096,8]{0,1:T(8,128)S(1)} all-gather(f32[512,8]{0,1:T(8,128)S(1)} %get-tuple-element.108), channel_id=2, replica_groups=mesh['lists'=64,'users'=8] {'users'}, dimensions={0}, use_global_device_ids=true | all-gather | bytes 147456 | tf_op jit(solution)/shard_map/all_gather | solution.py:10
  225.9 13.0 %all-gather.1 = f32[4096,8]{0,1:T(8,128)S(1)} all-gather(f32[512,8]{0,1:T(8,128)S(1)} %fusion.8), channel_id=3, replica_groups=mesh['lists'=64,'users'=8] {'users'}, dimensions={0}, use_global_device_ids=true | all-gather | bytes 147456 | tf_op jit(solution)/shard_map/all_gather | solution.py:10
  242.3 2.4 slice_bitcast_fusion
  244.6 2.0 copy.37
  246.6 6.5 %slice.66 = f32[3584,8,64]{0,2,1:T(8,128)} slice(f32[4096,8,64]{0,2,1:T(8,128)} %all-gather.5.cloned.1.call-done), slice={[512:4096], [0:8], [0:64]} | slice | bytes 14680064 | tf_op jit(solution)/shard_map/slice | solution.py:12
  253.1 11.2 %copy.41 = f32[3584,8,64]{2,1,0:T(8,128)} copy(f32[3584,8,64]{0,2,1:T(8,128)} %slice.66) | data formatting | bytes 14680064 | tf_op jit(solution)/shard_map/while | solution.py:13
  264.4 46.7 %while.2 = (s32[]{:T(128)}, f32[1,512,8]{1,2,0:T(8,128)S(1)}, f32[1,512,8]{1,2,0:T(8,128)S(1)}, f32[1,512,8,64]{3,2,1,0:T(8,128)S(1)}, f32[7,1,512,8]{2,3,1,0:T(...) while((s32[]{:T(128)}, f32[1,512,8]{1,2,0:T(8,128)S(1)}, ...), condition=%wide.region_11.12_spmd, body=%wide.region_10.11_spmd.sunk | while | flops 815106 | bytes 3457129 | solution.py:13
  266.8 4.2 %fusion.55 = f32[1,512,8,64]{3,2,1,0:T(8,128)S(1)} fusion(f32[7,1,512,8,64]{4,3,2,1,0:T(8,128)} %get-tuple-element.183, s32[]{:T(128)S(6)} %copy.57, f32[1,512,8,64]{3,2,1,0:T(8,128)S(1)} %get-tuple-element.172, f32[512,8]{1,0:T(8,128)} %copy.50, f32[512,8]{1,0:T(8,128)S(1)} %copy.51), kind=kLoop, calls=%fused_computation.6.clone.1 | loop fusion | flops 786432 | bytes 3178500 | tf_op jit(solution)/shard_map/while/body/eval_jaxpr/add | solution.py:32
  273.5 4.2 %fusion.55 = f32[1,512,8,64]{3,2,1,0:T(8,128)S(1)} fusion(f32[7,1,512,8,64]{4,3,2,1,0:T(8,128)} %get-tuple-element.183, s32[]{:T(128)S(6)} %copy.57, f32[1,512,8,64]{3,2,1,0:T(8,128)S(1)} %get-tuple-element.172, f32[512,8]{1,0:T(8,128)} %copy.50, f32[512,8]{1,0:T(8,128)S(1)} %copy.51), kind=kLoop, calls=%fused_computation.6.clone.1 | loop fusion | flops 786432 | bytes 3178500 | tf_op jit(solution)/shard_map/while/body/eval_jaxpr/add | solution.py:32
  280.2 4.2 %fusion.55 = f32[1,512,8,64]{3,2,1,0:T(8,128)S(1)} fusion(f32[7,1,512,8,64]{4,3,2,1,0:T(8,128)} %get-tuple-element.183, s32[]{:T(128)S(6)} %copy.57, f32[1,512,8,64]{3,2,1,0:T(8,128)S(1)} %get-tuple-element.172, f32[512,8]{1,0:T(8,128)} %copy.50, f32[512,8]{1,0:T(8,128)S(1)} %copy.51), kind=kLoop, calls=%fused_computation.6.clone.1 | loop fusion | flops 786432 | bytes 3178500 | tf_op jit(solution)/shard_map/while/body/eval_jaxpr/add | solution.py:32
  286.9 4.2 %fusion.55 = f32[1,512,8,64]{3,2,1,0:T(8,128)S(1)} fusion(f32[7,1,512,8,64]{4,3,2,1,0:T(8,128)} %get-tuple-element.183, s32[]{:T(128)S(6)} %copy.57, f32[1,512,8,64]{3,2,1,0:T(8,128)S(1)} %get-tuple-element.172, f32[512,8]{1,0:T(8,128)} %copy.50, f32[512,8]{1,0:T(8,128)S(1)} %copy.51), kind=kLoop, calls=%fused_computation.6.clone.1 | loop fusion | flops 786432 | bytes 3178500 | tf_op jit(solution)/shard_map/while/body/eval_jaxpr/add | solution.py:32
  293.6 4.2 %fusion.55 = f32[1,512,8,64]{3,2,1,0:T(8,128)S(1)} fusion(f32[7,1,512,8,64]{4,3,2,1,0:T(8,128)} %get-tuple-element.183, s32[]{:T(128)S(6)} %copy.57, f32[1,512,8,64]{3,2,1,0:T(8,128)S(1)} %get-tuple-element.172, f32[512,8]{1,0:T(8,128)} %copy.50, f32[512,8]{1,0:T(8,128)S(1)} %copy.51), kind=kLoop, calls=%fused_computation.6.clone.1 | loop fusion | flops 786432 | bytes 3178500 | tf_op jit(solution)/shard_map/while/body/eval_jaxpr/add | solution.py:32
  300.2 4.2 %fusion.55 = f32[1,512,8,64]{3,2,1,0:T(8,128)S(1)} fusion(f32[7,1,512,8,64]{4,3,2,1,0:T(8,128)} %get-tuple-element.183, s32[]{:T(128)S(6)} %copy.57, f32[1,512,8,64]{3,2,1,0:T(8,128)S(1)} %get-tuple-element.172, f32[512,8]{1,0:T(8,128)} %copy.50, f32[512,8]{1,0:T(8,128)S(1)} %copy.51), kind=kLoop, calls=%fused_computation.6.clone.1 | loop fusion | flops 786432 | bytes 3178500 | tf_op jit(solution)/shard_map/while/body/eval_jaxpr/add | solution.py:32
  306.9 4.2 %fusion.55 = f32[1,512,8,64]{3,2,1,0:T(8,128)S(1)} fusion(f32[7,1,512,8,64]{4,3,2,1,0:T(8,128)} %get-tuple-element.183, s32[]{:T(128)S(6)} %copy.57, f32[1,512,8,64]{3,2,1,0:T(8,128)S(1)} %get-tuple-element.172, f32[512,8]{1,0:T(8,128)} %copy.50, f32[512,8]{1,0:T(8,128)S(1)} %copy.51), kind=kLoop, calls=%fused_computation.6.clone.1 | loop fusion | flops 786432 | bytes 3178500 | tf_op jit(solution)/shard_map/while/body/eval_jaxpr/add | solution.py:32
  311.6 1.9 fusion.12
  (109 shorter events, 40.8 us)
Async XLA Ops:
  7.2 69.3 %copy-start = (bf16[512,1024]{1,0:T(8,128)(2,1)S(1)}, bf16[512,1024]{1,0:T(8,128)(2,1)}, u32[]{:S(2)}) copy-start(bf16[512,1024]{1,0:T(8,128)(2,1)} %param.18) | copy-start | bytes 3145732
  7.2 41.2 %copy-start.1 = (bf16[1,512,512]{2,1,0:T(8,128)(2,1)S(1)}, bf16[1,512,512]{2,1,0:T(8,128)(2,1)}, u32[]{:S(2)}) copy-start(bf16[1,512,512]{2,1,0:T(8,128)(2,1)} %param.13) | copy-start | bytes 1572868
  50.2 23.0 %all-to-all-start.3 = ((bf16[64,3,512]{2,1,0:T(4,128)(2,1)}), bf16[64,3,512]{2,1,0:T(4,128)(2,1)S(1)}, u32[]{:S(2)}, u32[]{:S(2)}) async-start(bf16[64,3,512]{2,1,0:T(4,128)(2,1)} %reshape.422), calls=%async_computation.3 | async-start | bytes 524288 | tf_op jit(solution)/shard_map/all_to_all | solution.py:91
  54.9 91.3 %all-reduce.2.cloned.1.call-start = ((), (), s32[]{:S(2)}) async-start(), calls=%async_computation.4 | async-start | bytes 1048576 | tf_op jit(solution)/shard_map/psum | solution.py:104
  73.4 3.1 copy-start.2
  75.4 70.8 %copy-start.8 = (bf16[512,512]{1,0:T(8,128)(2,1)S(1)}, bf16[512,512]{1,0:T(8,128)(2,1)}, u32[]{:S(2)}) copy-start(bf16[512,512]{1,0:T(8,128)(2,1)} %param.17) | copy-start | bytes 1572868
  76.4 165.8 %all-gather.5.cloned.1.call-start = ((), (), s32[]{:S(2)}) async-start(), calls=%async_computation.5 | async-start | bytes 9437184 | tf_op jit(solution)/shard_map/all_gather | solution.py:10
  77.0 71.3 %copy-start.3 = (pred[128]{0:T(512)(128)(4,1)}, pred[128]{0:T(512)(128)(4,1)S(1)}, u32[]{:S(2)}) copy-start(pred[128]{0:T(512)(128)(4,1)S(1)} %add_compare_fusion) | copy-start | bytes 388
  148.3 1.7 copy-start.5
  148.3 2.8 copy-start.6
  154.3 54.6 %copy-start.7 = (s32[128]{0:T(128)S(1)}, s32[128]{0:T(128)}, u32[]{:S(2)}) copy-start(s32[128]{0:T(128)} %fusion.38) | copy-start | bytes 1540
  197.4 27.9 %copy-start.4 = (pred[128]{0:T(512)(128)(4,1)S(1)}, pred[128]{0:T(512)(128)(4,1)}, u32[]{:S(2)}) copy-start(pred[128]{0:T(512)(128)(4,1)} %copy-done.3) | copy-start | bytes 388
  199.9 39.7 %all-to-all-start.1 = ((bf16[64,1,6,512]{3,2,1,0:T(8,128)(2,1)}), bf16[64,1,6,512]{3,2,1,0:T(8,128)(2,1)}, u32[]{:S(2)}, u32[]{:S(2)}) async-start(bf16[64,1,6,512]{3,2,1,0:T(8,128)(2,1)} %copy.32), calls=%async_computation.1 | async-start | bytes 1048576 | tf_op jit(solution)/shard_map/all_to_all | solution.py:69
Sparse Core Ops, SparseCore 0:
  76.6 69.6 all-reduce.1
  150.1 58.5 all-gather.4
where the time goes:
time: 327 us; the launch traced here: 320 us
  blocking collectives  104 us (32%)
  waiting for transfers between devices  86.9 us (27%)
  other arithmetic  48 us (15%)
  local copies, waits for them, and re-layouts  44.6 us (14%)
  between operations  15 us (5%)
  starting transfers between devices  13.8 us (4%)
  matrix products  7.35 us (2%)
    psum x1, waiting for transfers between devices, shards(): cand_rows = lax.psum(mine.astype(jnp.bfloat16), 'users')  69.2 us
    all_to_all x1, blocking collectives, shards(): lax.all_to_all(outgoing, 'lists', split_axis=0, concat_axis=0, tiled=True)  43.1 us
    all_to_all x1, blocking collectives, shards(): lax.all_to_all(request, 'lists', split_axis=0, concat_axis=0, tiled=True)  32.5 us
    add x7, other arithmetic, softmax_combine(): first[2] * left[..., None] + second[2] * right[..., None]  29.2 us
    all_gather x2, blocking collectives, merged(): pieces = jax.tree.map(lambda part: lax.all_gather(part, axis), value)  28.8 us
    all_to_all x1, waiting for transfers between devices, shards(): lax.all_to_all(flat_items[lax.all_to_all(request, 'lists', split_axis=0,...  17.7 us
    while x2, local copies, waits for them, and re-layouts, merged(): lax.scan(lambda running, share: (join(running, share), None), head, tail)  13.2 us
    all_to_all x1, starting transfers between devices, shards(): lax.all_to_all(scores, 'lists', split_axis=0, concat_axis=0, tiled=True)  9.07 us
  transfers between devices with their start and end apart: 4, of which 2 were waited for; matrix products, arithmetic and copies ran while one was open for 4% of the time, Pallas kernels for 0%

commit v1 on v0

v1 whole, which is shorter than its diff:
```python
import functools

import jax
import jax.numpy as jnp
from jax import lax
from jax.experimental import pallas as pl
from jax.experimental.pallas import tpu as pltpu
from jax.sharding import PartitionSpec as P

MESH = pl.DeviceIdType.MESH
F32 = jnp.float32
BF16 = jnp.bfloat16

L = 64
U = 8
X = 4
USERS = 4
PROBES = 32
ITEMS = 512
D = 512
SLOTS = 3
CANDS = 512
OWN = CANDS // U
EVENTS = 128
HIST = U * EVENTS
HEADS = 8
G = D // 128
ROWS = 16


def dot(a, b):
    return jnp.dot(a, b, preferred_element_type=F32)


def dot_first(a, b):
    return lax.dot_general(a, b, (((0,), (0,)), ((), ())), preferred_element_type=F32)


def dot_last(a, b):
    return lax.dot_general(a, b, (((1,), (1,)), ((), ())), preferred_element_type=F32)


def iota(shape, dim):
    return lax.broadcasted_iota(jnp.int32, shape, dim)


def kernel(
    ids,
    length,
    users,
    probes,
    items_hbm,
    history_hbm,
    wq_hbm,
    wkv_hbm,
    wo_hbm,
    list_scores,
    ranked,
    items,
    wq,
    wkv,
    wo,
    history,
    pairs,
    select,
    request,
    ask,
    asked,
    user_part,
    user_all,
    stage,
    rows_out,
    rows_in,
    scores_out,
    scores_in,
    placed,
    swap,
    spread,
    gathered,
    local_sem,
    send_sem,
    recv_sem,
):
    me = lax.axis_index("lists")
    col = lax.axis_index("users")
    chip, core = lax.div(col, 2), lax.rem(col, 2)

    def local(source, target, at):
        return pltpu.make_async_copy(source, target, local_sem.at[at])

    copies = [
        local(items_hbm, items, 0),
        local(history_hbm, history.at[col], 1),
        local(wkv_hbm, wkv, 2),
        local(wq_hbm, wq, 3),
        local(wo_hbm, wo, 4),
    ]
    for copy in copies:
        copy.start()

    barrier = pltpu.get_barrier_semaphore()

    @pl.loop(0, L)
    def _(p):
        @pl.when(p != me)
        def _():
            pl.semaphore_signal(barrier, inc=1, device_id=(p, col), device_id_type=MESH)

    @pl.loop(1, U)
    def _(d):
        pl.semaphore_signal(
            barrier, inc=1, device_id=(me, lax.rem(col + d, U)), device_id_type=MESH
        )

    wanted = ids[...]
    mine = lax.shift_right_logical(wanted, 9) == iota((L, CANDS), 0) * U + col
    mine = jnp.where(mine, 1.0, 0.0).astype(F32)
    place = jnp.bitwise_and(wanted, ITEMS - 1).astype(F32)
    earlier = jnp.where(iota((CANDS, CANDS), 0) < iota((CANDS, CANDS), 1), 1.0, 0.0)
    before = dot(mine.astype(BF16), earlier.astype(BF16))
    lane = iota((L, 128), 1)
    line = jnp.zeros((L, 128), F32)
    for k in range(SLOTS):
        chosen = jnp.where(before == k, mine, 0.0)
        select[k * L : (k + 1) * L, :] = chosen.astype(BF16)
        line = jnp.where(lane == k, jnp.sum(chosen * place, axis=1, keepdims=True), line)
    request[...] = line
    vectors = users[...].astype(F32)
    half = jnp.where(core == 0, vectors[:, :256], vectors[:, 256:])
    part = jnp.sum(jnp.where(iota((USERS, 256), 0) == chip, half, 0.0), axis=0, keepdims=True)

    @pl.loop(0, L)
    def _(p):
        ask[p, :, 0:128] = request[pl.ds(p, 1), :]
        ask[p, :, 128:384] = part

    stage[...] = jnp.zeros_like(stage)
    pl.semaphore_wait(barrier, L - 1 + U - 1)

    def to_rows(source, target, at):
        @pl.loop(1, L)
        def _(d):
            p = lax.rem(me + d, L)
            pltpu.make_async_remote_copy(
                source.at[p],
                target.at[me],
                send_sem.at[at],
                recv_sem.at[at],
                device_id=(p, col),
                device_id_type=MESH,
            ).start()

    def to_columns(source, target, at):
        @pl.loop(1, U)
        def _(d):
            pltpu.make_async_remote_copy(
                source,
                target.at[col],
                send_sem.at[at],
                recv_sem.at[at],
                device_id=(me, lax.rem(col + d, U)),
                device_id_type=MESH,
            ).start()

    def wait_all(target, count, sem):
        some = target.at[pl.ds(0, count)]
        pltpu.make_async_copy(some, some, sem).wait()

    to_rows(ask, asked, 0)
    copies[1].wait()
    to_columns(history.at[col], history, 1)
    asked[me] = ask[me]
    wait_all(asked, L - 1, recv_sem.at[0])

    @pl.loop(0, L)
    def _(p):
        request[pl.ds(p, 1), :] = asked[p, :, 0:128]
        user_part[pl.ds(p, 1), :] = asked[p, :, 128:384]

    user_all[col] = user_part[...].astype(BF16)
    to_columns(user_all.at[col], user_all, 2)

    copies[0].wait()
    asks = request[...]
    for k in range(SLOTS):
        hot = jnp.where(asks[:, k : k + 1] == iota((L, ITEMS), 1).astype(F32), 1.0, 0.0)
        found = dot(hot.astype(BF16), items[...])
        for g in range(G):
            stage[pl.ds(k * G + g, L, stride=ROWS), :] = found[:, g * 128 : (g + 1) * 128]
    rows_out[...] = stage[...].reshape(L, ROWS, 128).astype(BF16)
    rows_in[me] = rows_out[me]
    to_rows(rows_out, rows_in, 3)

    wait_all(user_all, U - 1, recv_sem.at[2])
    for u in range(USERS):
        found = dot_last(user_all[2 * u], items[:, 0:256]) + dot_last(
            user_all[2 * u + 1], items[:, 256:512]
        )
        found = found * D ** (-0.5)
        for g in range(G):
            stage[pl.ds(u * G + g, L, stride=ROWS), :] = found[:, g * 128 : (g + 1) * 128]
    scores_out[...] = stage[...].reshape(L, ROWS, 128).astype(BF16)
    scores_in[me] = scores_out[me]
    to_rows(scores_out, scores_in, 4)

    for copy in copies[2:]:
        copy.wait()
    wait_all(history, U - 1, recv_sem.at[1])

    @pl.loop(0, U)
    def _(c):
        pairs[pl.ds(pl.multiple_of(c * EVENTS, EVENTS), EVENTS), :] = dot(
            history[c], wkv[...]
        ).astype(BF16)

    wait_all(rows_in, L - 1, recv_sem.at[3])
    stage[...] = rows_in[...].astype(F32).reshape(L * ROWS, 128)
    for k in range(SLOTS):
        for g in range(G):
            gathered[k * L : (k + 1) * L, g * 128 : (g + 1) * 128] = stage[
                pl.ds(k * G + g, L, stride=ROWS), :
            ].astype(BF16)
    spots = dot_first(select[...], gathered[...]).astype(BF16)
    for c in range(U):
        placed[c % 2, c // 2] = spots[c * OWN : (c + 1) * OWN, :]
    first = pltpu.make_async_remote_copy(
        placed.at[1 - core],
        swap,
        send_sem.at[5],
        recv_sem.at[5],
        device_id=(me, 2 * chip + 1 - core),
        device_id_type=MESH,
    )
    first.start()
    first.wait_recv()
    spread[0:X] = (placed[core].astype(F32) + swap[...].astype(F32)).astype(BF16)

    @pl.loop(1, X)
    def _(d):
        there = lax.rem(chip + d, X)
        pltpu.make_async_remote_copy(
            spread.at[there],
            spread.at[X + d],
            send_sem.at[6],
            recv_sem.at[6],
            device_id=(me, 2 * there + core),
            device_id_type=MESH,
        ).start()

    wait_all(spread, X - 1, recv_sem.at[6])
    cand = spread[chip].astype(F32)
    for d in range(1, X):
        cand = cand + spread[X + d].astype(F32)

    queries = (dot(cand.astype(BF16), wq[...]) * (D // HEADS) ** (-0.5)).astype(BF16)
    low = iota((OWN, 128), 1) < 64
    valid = iota((1, HIST), 1) < length[0]
    nothing = jnp.zeros((OWN, 128), BF16)
    attended = []
    for j in range(HEADS // 2):
        two = queries[:, j * 128 : (j + 1) * 128]
        two = jnp.concatenate([jnp.where(low, two, nothing), jnp.where(low, nothing, two)], axis=0)
        scores = dot_last(two, pairs[:, j * 128 : (j + 1) * 128])
        scores = jnp.where(valid, scores, F32(-1e30))
        top = jnp.max(scores, axis=1, keepdims=True)
        powers = jnp.where(valid, jnp.exp(scores - top), 0.0)
        total = jnp.sum(powers, axis=1, keepdims=True)
        mixed = dot(powers.astype(BF16), pairs[:, D + j * 128 : D + (j + 1) * 128]) / total
        attended.append(jnp.where(low, mixed[:OWN], mixed[OWN:]).astype(BF16))
    ranked[...] = dot(jnp.concatenate(attended, axis=1), wo[...]).astype(BF16)

    wait_all(scores_in, L - 1, recv_sem.at[4])
    stage[...] = scores_in[...].astype(F32).reshape(L * ROWS, 128)
    for u in range(USERS):
        hot = jnp.where(iota((L, PROBES), 0) == probes[u : u + 1, :], 1.0, 0.0).astype(BF16)
        for g in range(G):
            found = stage[pl.ds(u * G + g, L, stride=ROWS), :].astype(BF16)
            list_scores[u, :, g * 128 : (g + 1) * 128] = dot_first(hot, found).astype(BF16)

    wait_all(asked, L - 1, send_sem.at[0])
    wait_all(history, U - 1, send_sem.at[1])
    wait_all(user_all, U - 1, send_sem.at[2])
    wait_all(rows_in, L - 1, send_sem.at[3])
    wait_all(scores_in, L - 1, send_sem.at[4])
    first.wait_send()
    wait_all(spread, X - 1, send_sem.at[6])


def shards(
    user_vectors,
    probe_lists,
    list_items,
    candidate_ids,
    history,
    history_lengths,
    query_weight,
    key_value_weight,
    out_weight,
):
    vmem = pl.BlockSpec(memory_space=pltpu.VMEM)
    smem = pl.BlockSpec(memory_space=pltpu.SMEM)
    hbm = pl.BlockSpec(memory_space=pl.ANY)
    list_scores, ranked = pl.pallas_call(
        kernel,
        out_shape=(
            jax.ShapeDtypeStruct((USERS, PROBES, ITEMS), BF16),
            jax.ShapeDtypeStruct((OWN, D), BF16),
        ),
        in_specs=[vmem, smem, vmem, vmem, hbm, hbm, hbm, hbm, hbm],
        out_specs=(vmem, vmem),
        scratch_shapes=[
            pltpu.VMEM((ITEMS, D), BF16),
            pltpu.VMEM((D, D), BF16),
            pltpu.VMEM((D, 2 * D), BF16),
            pltpu.VMEM((D, D), BF16),
            pltpu.VMEM((U, EVENTS, D), BF16),
            pltpu.VMEM((HIST, 2 * D), BF16),
            pltpu.VMEM((SLOTS * L, CANDS), BF16),
            pltpu.VMEM((L, 128), F32),
            pltpu.VMEM((L, 1, 384), F32),
            pltpu.VMEM((L, 1, 384), F32),
            pltpu.VMEM((L, 256), F32),
            pltpu.VMEM((U, L, 256), BF16),
            pltpu.VMEM((L * ROWS, 128), F32),
            pltpu.VMEM((L, ROWS, 128), BF16),
            pltpu.VMEM((L, ROWS, 128), BF16),
            pltpu.VMEM((L, ROWS, 128), BF16),
            pltpu.VMEM((L, ROWS, 128), BF16),
            pltpu.VMEM((2, X, OWN, D), BF16),
            pltpu.VMEM((X, OWN, D), BF16),
            pltpu.VMEM((2 * X, OWN, D), BF16),
            pltpu.VMEM((SLOTS * L, D), BF16),
            pltpu.SemaphoreType.DMA((5,)),
            pltpu.SemaphoreType.DMA((7,)),
            pltpu.SemaphoreType.DMA((7,)),
        ],
        compiler_params=pltpu.CompilerParams(
            collective_id=0, has_side_effects=True, vmem_limit_bytes=56 * 2**20
        ),
        cost_estimate=pl.CostEstimate(
            flops=2 * 10**9, bytes_accessed=4 * 10**6, transcendentals=600000
        ),
    )(
        candidate_ids,
        history_lengths,
        user_vectors,
        probe_lists,
        list_items.reshape(ITEMS, D),
        history.reshape(EVENTS, D),
        query_weight,
        key_value_weight,
        out_weight,
    )
    return list_scores, ranked.reshape(1, OWN, D)


def solution(mesh):
    placed = (
        P("lists", None),
        P("lists", None),
        P("lists", "users", None),
        P("lists", None),
        P("lists", "users", None),
        P("lists"),
        P(),
        P(),
        P(),
    )
    return jax.shard_map(
        shards,
        mesh=mesh,
        in_specs=placed,
        out_specs=(P("lists", None, "users"), P("lists", "users", None)),
        check_vma=False,
    )
```

time: 327 us -> 60.2 us (0.18)
  the two profiles are of different devices: /device:TPU:1 before, /device:TPU:65 now
where the time goes in v1:
time: 60.2 us; the launch traced here: 60 us
  Pallas kernels  56.5 us (94%)
  local copies, waits for them, and re-layouts  2.23 us (4%)
  between operations  1.29 us (2%)
    pallas_call x1, Pallas kernels, shards(): pl.pallas_call(kernel, out_shape=(jax.ShapeDtypeStruct((USERS, PROBES, IT...  56.5 us
    unnamed x4, local copies, waits for them, and re-layouts  2.23 us

profile of v1, /device:TPU:65, one launch (start us, length us, event | category | flops | bytes accessed | tf_op | source)
XLA Modules:
  0.0 60.0 jit_solution(19350666035943127)
XLA Ops:
  1.3 56.5 %shard_map.104 = (bf16[4,32,512]{2,1,0:T(8,128)(2,1)}, bf16[64,512]{1,0:T(8,128)(2,1)}) custom-call(s32[1,512]{1,0:T(1,128)} %ids.1, s32[1]{0:T(128)S(6)} %copy.13.length, bf16[4,512]{1,0:T(4,128)(2,1)} %users.1, s32[4,32]{1,0:T(4,128)} %probes.1, bf16[512,512]{1,0:T(8,128)(2,1)} %bitcast.4, bf16[128,512]{1,0:T(8,128)(2,1)} %bitcast.5, ...), custom_call_target="tpu_custom_call" | custom-call | flops 2000000000 | bytes 4000000 | tf_op jit(solution)/shard_map/pallas_call | solution.py:303
  57.8 0.0 copy-start
  57.8 1.6 %copy.14 = bf16[4,32,512]{2,1,0:T(8,128)(2,1)} copy(bf16[4,32,512]{2,1,0:T(8,128)(2,1)} %get-tuple-element.8) | data formatting | bytes 262144
  59.4 0.0 copy-done
  59.4 0.6 %copy.15 = bf16[1,64,512]{2,1,0:T(8,128)(2,1)} copy(bf16[1,64,512]{2,1,0:T(8,128)(2,1)S(1)} %bitcast.3) | data formatting | bytes 131072
Async XLA Ops:
  57.8 1.6 %copy-start = (bf16[64,512]{1,0:T(8,128)(2,1)S(1)}, bf16[64,512]{1,0:T(8,128)(2,1)}, u32[]{:S(2)}) copy-start(bf16[64,512]{1,0:T(8,128)(2,1)} %get-tuple-element.5) | copy-start | bytes 196612

commit v2 on v1

v2 whole, which is shorter than its diff:
```python
import jax
import jax.numpy as jnp
from jax import lax
from jax.experimental import pallas as pl
from jax.experimental.pallas import tpu as pltpu
from jax.sharding import PartitionSpec as P

MESH = pl.DeviceIdType.MESH
F32 = jnp.float32
BF16 = jnp.bfloat16

L = 64
U = 8
X = 4
USERS = 4
PROBES = 32
ITEMS = 512
D = 512
SLOTS = 3
CANDS = 512
OWN = CANDS // U
EVENTS = 128
HIST = U * EVENTS
HEADS = 8
G = D // 128
ROWS = 16


def dot(a, b):
    return jnp.dot(a, b, preferred_element_type=F32)


def dot_first(a, b):
    return lax.dot_general(a, b, (((0,), (0,)), ((), ())), preferred_element_type=F32)


def dot_last(a, b):
    return lax.dot_general(a, b, (((1,), (1,)), ((), ())), preferred_element_type=F32)


def iota(shape, dim):
    return lax.broadcasted_iota(jnp.int32, shape, dim)


def kernel(
    ids_hbm,
    length_hbm,
    users_hbm,
    items_hbm,
    history_hbm,
    wq_hbm,
    wkv_hbm,
    wo_hbm,
    scores_in,
    ranked,
    ids,
    length,
    users,
    items,
    wq,
    wkv,
    wo,
    history,
    pairs,
    select,
    request,
    ask,
    asked,
    part,
    parts,
    user_part,
    user_all,
    stage,
    rows_out,
    rows_in,
    scores_out,
    placed,
    swap,
    spread,
    gathered,
    local_sem,
    send_sem,
    recv_sem,
):
    me = lax.axis_index("lists")
    col = lax.axis_index("users")
    chip, core = lax.div(col, 2), lax.rem(col, 2)

    def local(source, target, at):
        return pltpu.make_async_copy(source, target, local_sem.at[at])

    get_ids = local(ids_hbm, ids, 0)
    get_users = local(users_hbm, users, 1)
    get_history = local(history_hbm, history.at[col], 2)
    get_items = local(items_hbm, items, 3)
    get_rest = [
        local(wkv_hbm, wkv, 4),
        local(wq_hbm, wq, 5),
        local(wo_hbm, wo, 6),
        local(length_hbm, length, 7),
    ]
    get_ids.start()
    get_users.start()
    get_history.start()

    barrier = pltpu.get_barrier_semaphore()

    @pl.loop(0, L)
    def _(p):
        @pl.when(p != me)
        def _():
            pl.semaphore_signal(barrier, inc=1, device_id=(p, col), device_id_type=MESH)

    @pl.loop(1, U)
    def _(d):
        pl.semaphore_signal(
            barrier, inc=1, device_id=(me, lax.rem(col + d, U)), device_id_type=MESH
        )

    get_items.start()
    for copy in get_rest:
        copy.start()

    get_ids.wait()
    wanted = ids[...]
    mine = lax.shift_right_logical(wanted, 9) == iota((L, CANDS), 0) * U + col
    mine = jnp.where(mine, 1.0, 0.0).astype(F32)
    place = jnp.bitwise_and(wanted, ITEMS - 1).astype(F32)
    earlier = jnp.where(iota((CANDS, CANDS), 0) < iota((CANDS, CANDS), 1), 1.0, 0.0)
    before = dot(mine.astype(BF16), earlier.astype(BF16))
    lane = iota((L, 128), 1)
    line = jnp.zeros((L, 128), F32)
    slots = []
    for k in range(SLOTS):
        slots.append(jnp.where(before == k, mine, 0.0))
        line = jnp.where(lane == k, jnp.sum(slots[k] * place, axis=1, keepdims=True), line)
    request[...] = line

    @pl.loop(0, L)
    def _(p):
        ask[p] = request[pl.ds(p, 1), :]

    get_users.wait()
    vectors = users[...].astype(F32)
    half = jnp.where(core == 0, vectors[:, :256], vectors[:, 256:])
    part[0] = jnp.sum(jnp.where(iota((USERS, 256), 0) == chip, half, 0.0), axis=0, keepdims=True)
    get_history.wait()
    pl.semaphore_wait(barrier, L - 1 + U - 1)

    def to_rows(source, target, at, order):
        def send(p):
            pltpu.make_async_remote_copy(
                source(p),
                target.at[me],
                send_sem.at[at],
                recv_sem.at[at],
                device_id=(p, col),
                device_id_type=MESH,
            ).start()

        if order is None:

            @pl.loop(1, L)
            def _(d):
                send(lax.rem(me + d, L))

        else:
            for first, count, rotate in order:
                @pl.loop(0, 4 * count)
                def _(i):
                    if rotate:
                        i = lax.rem(i + me + 4 * rotate, 4 * count)
                    p = 4 * first + i
                    @pl.when(p != me)
                    def _():
                        send(p)

    def to_chips(source, target, at):
        @pl.loop(1, X)
        def _(d):
            there = lax.rem(chip + d, X)
            pltpu.make_async_remote_copy(
                source(there),
                target(d),
                send_sem.at[at],
                recv_sem.at[at],
                device_id=(me, 2 * there + core),
                device_id_type=MESH,
            ).start()

    def to_core(source, target, at):
        return pltpu.make_async_remote_copy(
            source,
            target,
            send_sem.at[at],
            recv_sem.at[at],
            device_id=(me, 2 * chip + 1 - core),
            device_id_type=MESH,
        )

    def wait_all(target, count, sem):
        some = target.at[pl.ds(0, count)]
        pltpu.make_async_copy(some, some, sem).wait()

    to_rows(lambda p: ask.at[p], asked, 0, None)
    to_chips(lambda there: history.at[col], lambda d: history.at[col], 1)
    to_rows(lambda p: part.at[0], parts, 2, None)
    asked[me] = ask[me]
    parts[me] = part[0]

    turned = jnp.concatenate(slots + [jnp.zeros((L, CANDS), F32)], axis=0).T.astype(BF16)
    for c in range(U):
        at = (c % 2) * X + c // 2
        select[at * OWN : (at + 1) * OWN, :] = turned[c * OWN : (c + 1) * OWN, :]
    gathered[SLOTS * L :, :] = jnp.zeros((L, D), BF16)
    stage[...] = jnp.zeros_like(stage)

    get_items.wait()
    wait_all(asked, L - 1, recv_sem.at[0])

    @pl.loop(0, L)
    def _(p):
        request[pl.ds(p, 1), :] = asked[p]

    asks = request[...]
    for k in range(SLOTS):
        hot = jnp.where(asks[:, k : k + 1] == iota((L, ITEMS), 1).astype(F32), 1.0, 0.0)
        found = dot(hot.astype(BF16), items[...])
        for g in range(G):
            stage[pl.ds(k * G + g, L, stride=ROWS), :] = found[:, g * 128 : (g + 1) * 128]
    rows_out[...] = stage[...].reshape(L, ROWS, 128).astype(BF16)
    to_rows(lambda p: rows_out.at[p], rows_in, 3, [(0, 4, 1), (4, 4, 1), (12, 4, 1), (8, 4, 1)])
    rows_in[me] = rows_out[me]

    wait_all(parts, L - 1, recv_sem.at[2])

    @pl.loop(0, L)
    def _(p):
        user_part[pl.ds(p, 1), :] = parts[p]

    user_all[col] = user_part[...].astype(BF16)

    @pl.loop(1, U)
    def _(d):
        pltpu.make_async_remote_copy(
            user_all.at[col],
            user_all.at[col],
            send_sem.at[4],
            recv_sem.at[4],
            device_id=(me, lax.rem(col + d, U)),
            device_id_type=MESH,
        ).start()

    wait_all(history, X - 1, recv_sem.at[1])

    @pl.loop(0, X)
    def _(x):
        to_core(history.at[2 * x + core], history.at[2 * x + core], 5).start()

    for copy in get_rest:
        copy.wait()
    wait_all(history, X, recv_sem.at[5])

    @pl.loop(0, U)
    def _(c):
        pairs[pl.ds(pl.multiple_of(c * EVENTS, EVENTS), EVENTS), :] = dot(
            history[c], wkv[...]
        ).astype(BF16)

    wait_all(user_all, U - 1, recv_sem.at[4])
    for u in range(USERS):
        found = dot_last(user_all[2 * u], items[:, 0:256]) + dot_last(
            user_all[2 * u + 1], items[:, 256:512]
        )
        found = found * D ** (-0.5)
        for g in range(G):
            stage[pl.ds(u * G + g, L, stride=ROWS), :] = found[:, g * 128 : (g + 1) * 128]
    scores_out[...] = stage[...].reshape(L, ROWS, 128).astype(BF16)
    keep = local(scores_out.at[me], scores_in.at[me], 8)
    keep.start()
    to_rows(lambda p: scores_out.at[p], scores_in, 6, None)

    wait_all(rows_in, L - 1, recv_sem.at[3])
    stage[...] = rows_in[...].astype(F32).reshape(L * ROWS, 128)
    for k in range(SLOTS):
        for g in range(G):
            gathered[k * L : (k + 1) * L, g * 128 : (g + 1) * 128] = stage[
                pl.ds(k * G + g, L, stride=ROWS), :
            ].astype(BF16)

    def spots(c):
        block = select[pl.ds(pl.multiple_of(c * X * OWN, X * OWN), X * OWN), :]
        return dot(block, gathered[...])

    placed[...] = spots(1 - core).astype(BF16).reshape(X, OWN, D)
    pair = to_core(placed, swap, 7)
    pair.start()
    kept = spots(core).reshape(X, OWN, D)
    pair.wait_recv()
    spread[0:X] = (kept + swap[...].astype(F32)).astype(BF16)
    to_chips(lambda there: spread.at[there], lambda d: spread.at[X + d], 8)
    wait_all(spread, X - 1, recv_sem.at[8])
    cand = spread[chip].astype(F32)
    for d in range(1, X):
        cand = cand + spread[X + d].astype(F32)

    queries = (dot(cand.astype(BF16), wq[...]) * (D // HEADS) ** (-0.5)).astype(BF16)
    low = iota((OWN, 128), 1) < 64
    valid = iota((1, HIST), 1) < length[0]
    nothing = jnp.zeros((OWN, 128), BF16)
    attended = []
    for j in range(HEADS // 2):
        two = queries[:, j * 128 : (j + 1) * 128]
        two = jnp.concatenate([jnp.where(low, two, nothing), jnp.where(low, nothing, two)], axis=0)
        scores = dot_last(two, pairs[:, j * 128 : (j + 1) * 128])
        scores = jnp.where(valid, scores, F32(-1e30))
        top = jnp.max(scores, axis=1, keepdims=True)
        powers = jnp.where(valid, jnp.exp(scores - top), 0.0)
        total = jnp.sum(powers, axis=1, keepdims=True)
        mixed = dot(powers.astype(BF16), pairs[:, D + j * 128 : D + (j + 1) * 128]) / total
        attended.append(jnp.where(low, mixed[:OWN], mixed[OWN:]).astype(BF16))
    ranked[...] = dot(jnp.concatenate(attended, axis=1), wo[...]).astype(BF16)

    wait_all(asked, L - 1, send_sem.at[0])
    wait_all(history, X - 1, send_sem.at[1])
    wait_all(parts, L - 1, send_sem.at[2])
    wait_all(rows_in, L - 1, send_sem.at[3])
    wait_all(user_all, U - 1, send_sem.at[4])
    wait_all(history, X, send_sem.at[5])
    pair.wait_send()
    wait_all(spread, X - 1, send_sem.at[8])
    keep.wait()
    wait_all(scores_in, L - 1, send_sem.at[6])
    wait_all(scores_in, L - 1, recv_sem.at[6])


def finish(
    probes_hbm, scores_hbm, ranked_hbm, list_scores, ranked, probes, scores, stage, sem
):
    copies = [
        pltpu.make_async_copy(scores_hbm, scores, sem.at[0]),
        pltpu.make_async_copy(probes_hbm, probes, sem.at[1]),
        pltpu.make_async_copy(ranked_hbm, ranked, sem.at[2]),
    ]
    for copy in copies:
        copy.start()
    copies[1].wait()
    copies[0].wait()
    stage[...] = scores[...].astype(F32).reshape(L * ROWS, 128)
    for u in range(USERS):
        hot = jnp.where(iota((L, PROBES), 0) == probes[u : u + 1, :], 1.0, 0.0).astype(BF16)
        found = [stage[pl.ds(u * G + g, L, stride=ROWS), :].astype(BF16) for g in range(G)]
        list_scores[u] = dot_first(hot, jnp.concatenate(found, axis=1)).astype(BF16)
    copies[2].wait()


def shards(
    user_vectors,
    probe_lists,
    list_items,
    candidate_ids,
    history,
    history_lengths,
    query_weight,
    key_value_weight,
    out_weight,
):
    vmem = pl.BlockSpec(memory_space=pltpu.VMEM)
    hbm = pl.BlockSpec(memory_space=pl.ANY)
    scores_in, ranked = pl.pallas_call(
        kernel,
        out_shape=(
            jax.ShapeDtypeStruct((L, ROWS, 128), BF16),
            jax.ShapeDtypeStruct((OWN, D), BF16),
        ),
        in_specs=[hbm] * 8,
        out_specs=(hbm, vmem),
        scratch_shapes=[
            pltpu.VMEM((1, CANDS), jnp.int32),
            pltpu.SMEM((1,), jnp.int32),
            pltpu.VMEM((USERS, D), BF16),
            pltpu.VMEM((ITEMS, D), BF16),
            pltpu.VMEM((D, D), BF16),
            pltpu.VMEM((D, 2 * D), BF16),
            pltpu.VMEM((D, D), BF16),
            pltpu.VMEM((U, EVENTS, D), BF16),
            pltpu.VMEM((HIST, 2 * D), BF16),
            pltpu.VMEM((CANDS, 4 * L), BF16),
            pltpu.VMEM((L, 128), F32),
            pltpu.VMEM((L, 1, 128), F32),
            pltpu.VMEM((L, 1, 128), F32),
            pltpu.VMEM((1, 1, 256), F32),
            pltpu.VMEM((L, 1, 256), F32),
            pltpu.VMEM((L, 256), F32),
            pltpu.VMEM((U, L, 256), BF16),
            pltpu.VMEM((L * ROWS, 128), F32),
            pltpu.VMEM((L, ROWS, 128), BF16),
            pltpu.VMEM((L, ROWS, 128), BF16),
            pltpu.VMEM((L, ROWS, 128), BF16),
            pltpu.VMEM((X, OWN, D), BF16),
            pltpu.VMEM((X, OWN, D), BF16),
            pltpu.VMEM((2 * X, OWN, D), BF16),
            pltpu.VMEM((4 * L, D), BF16),
            pltpu.SemaphoreType.DMA((9,)),
            pltpu.SemaphoreType.DMA((9,)),
            pltpu.SemaphoreType.DMA((9,)),
        ],
        compiler_params=pltpu.CompilerParams(
            collective_id=0, has_side_effects=True, vmem_limit_bytes=56 * 2**20
        ),
        cost_estimate=pl.CostEstimate(
            flops=2 * 10**9, bytes_accessed=4 * 10**6, transcendentals=600000
        ),
    )(
        candidate_ids,
        history_lengths,
        user_vectors,
        list_items.reshape(ITEMS, D),
        history.reshape(EVENTS, D),
        query_weight,
        key_value_weight,
        out_weight,
    )
    list_scores, ranked = pl.pallas_call(
        finish,
        out_shape=(
            jax.ShapeDtypeStruct((USERS, PROBES, ITEMS), BF16),
            jax.ShapeDtypeStruct((OWN, D), BF16),
        ),
        in_specs=[hbm] * 3,
        out_specs=(vmem, vmem),
        scratch_shapes=[
            pltpu.VMEM((USERS, PROBES), jnp.int32),
            pltpu.VMEM((L, ROWS, 128), BF16),
            pltpu.VMEM((L * ROWS, 128), F32),
            pltpu.SemaphoreType.DMA((3,)),
        ],
        compiler_params=pltpu.CompilerParams(vmem_limit_bytes=56 * 2**20),
        cost_estimate=pl.CostEstimate(flops=2 * 10**7, bytes_accessed=10**6, transcendentals=0),
    )(probe_lists, scores_in, ranked)
    return list_scores, ranked.reshape(1, OWN, D)


def solution(mesh):
    placed = (
        P("lists", None),
        P("lists", None),
        P("lists", "users", None),
        P("lists", None),
        P("lists", "users", None),
        P("lists"),
        P(),
        P(),
        P(),
    )
    return jax.shard_map(
        shards,
        mesh=mesh,
        in_specs=placed,
        out_specs=(P("lists", None, "users"), P("lists", "users", None)),
        check_vma=False,
    )
```

time: 60.2 us -> 55.9 us (0.929)
  the two profiles are of different devices: /device:TPU:65 before, /device:TPU:1 now
where the time goes in v2:
time: 55.9 us; the launch traced here: 55.7 us
  Pallas kernels  54.4 us (97%)
  between operations  1.29 us (2%)
    pallas_call x1, Pallas kernels, shards(): pl.pallas_call(kernel, out_shape=(jax.ShapeDtypeStruct((L, ROWS, 128), BF...  52.4 us
    pallas_call x1, Pallas kernels, shards(): pl.pallas_call(finish, out_shape=(jax.ShapeDtypeStruct((USERS, PROBES, IT...  1.98 us

profile of v2, /device:TPU:1, one launch (start us, length us, event | category | flops | bytes accessed | tf_op | source)
XLA Modules:
  0.0 55.7 jit_solution(18142837651680909401)
XLA Ops:
  1.3 52.4 %shard_map.104 = (bf16[64,16,128]{2,1,0:T(8,128)(2,1)}, bf16[64,512]{1,0:T(8,128)(2,1)}) custom-call(s32[1,512]{1,0:T(1,128)} %ids_hbm.1, s32[1]{0:T(128)S(6)} %copy.11.length_hbm, bf16[4,512]{1,0:T(4,128)(2,1)} %users_hbm.1, bf16[512,512]{1,0:T(8,128)(2,1)} %bitcast.3, bf16[128,512]{1,0:T(8,128)(2,1)} %bitcast.4, bf16[512,512]{1,0:T(8,128)(2,1)} %wq_hbm.1, ...), custom_call_target="tpu_custom_call" | custom-call | flops 2000000000 | bytes 4000000 | tf_op jit(solution)/shard_map/pallas_call | solution.py:370
  53.7 2.0 %shard_map.105 = (bf16[4,32,512]{2,1,0:T(8,128)(2,1)}, bf16[64,512]{1,0:T(8,128)(2,1)}) custom-call(s32[4,32]{1,0:T(4,128)} %probes_hbm.1, bf16[64,16,128]{2,1,0:T(8,128)(2,1)} %get-tuple-element.6.scores_hbm, bf16[64,512]{1,0:T(8,128)(2,1)} %get-tuple-element.7.ranked_hbm), custom_call_target="tpu_custom_call" | custom-call | flops 20000000 | bytes 1000000 | tf_op jit(solution)/shard_map/pallas_call | solution.py:424

commit v3 on v2

--- a/solution.py
+++ b/solution.py
@@ -10,6 +10,7 @@
 BF16 = jnp.bfloat16
 
 L = 64
+Z = 16
 U = 8
 X = 4
 USERS = 4
@@ -69,6 +70,7 @@
     part,
     parts,
     user_part,
+    user_plane,
     user_all,
     stage,
     rows_out,
@@ -81,10 +83,12 @@
     local_sem,
     send_sem,
     recv_sem,
+    heard,
 ):
     me = lax.axis_index("lists")
     col = lax.axis_index("users")
     chip, core = lax.div(col, 2), lax.rem(col, 2)
+    plane, row = lax.div(me, 4), lax.rem(me, 4)
 
     def local(source, target, at):
         return pltpu.make_async_copy(source, target, local_sem.at[at])
@@ -105,11 +109,16 @@
 
     barrier = pltpu.get_barrier_semaphore()
 
-    @pl.loop(0, L)
-    def _(p):
-        @pl.when(p != me)
-        def _():
-            pl.semaphore_signal(barrier, inc=1, device_id=(p, col), device_id_type=MESH)
+    def over_z(d):
+        return lax.rem(me + 4 * d, L)
+
+    def over_y(d):
+        return me - row + lax.rem(row + d, 4)
+
+    for d in range(1, Z):
+        pl.semaphore_signal(barrier, inc=1, device_id=(over_z(d), col), device_id_type=MESH)
+    for d in range(1, 4):
+        pl.semaphore_signal(barrier, inc=1, device_id=(over_y(d), col), device_id_type=MESH)
 
     @pl.loop(1, U)
     def _(d):
@@ -145,7 +154,10 @@
     half = jnp.where(core == 0, vectors[:, :256], vectors[:, 256:])
     part[0] = jnp.sum(jnp.where(iota((USERS, 256), 0) == chip, half, 0.0), axis=0, keepdims=True)
     get_history.wait()
-    pl.semaphore_wait(barrier, L - 1 + U - 1)
+    pl.semaphore_wait(barrier, Z - 1 + 4 - 1 + U - 1)
+    for d in range(1, 4):
+        pl.semaphore_signal(heard, inc=1, device_id=(over_y(d), col), device_id_type=MESH)
+    pl.semaphore_wait(heard, 4 - 1)
 
     def to_rows(source, target, at, order):
         def send(p):
@@ -204,9 +216,17 @@
 
     to_rows(lambda p: ask.at[p], asked, 0, None)
     to_chips(lambda there: history.at[col], lambda d: history.at[col], 1)
-    to_rows(lambda p: part.at[0], parts, 2, None)
+    for d in range(1, Z):
+        pltpu.make_async_remote_copy(
+            part.at[0],
+            parts.at[plane],
+            send_sem.at[2],
+            recv_sem.at[2],
+            device_id=(over_z(d), col),
+            device_id_type=MESH,
+        ).start()
     asked[me] = ask[me]
-    parts[me] = part[0]
+    parts[plane] = part[0]
 
     turned = jnp.concatenate(slots + [jnp.zeros((L, CANDS), F32)], axis=0).T.astype(BF16)
     for c in range(U):
@@ -229,16 +249,31 @@
         for g in range(G):
             stage[pl.ds(k * G + g, L, stride=ROWS), :] = found[:, g * 128 : (g + 1) * 128]
     rows_out[...] = stage[...].reshape(L, ROWS, 128).astype(BF16)
-    to_rows(lambda p: rows_out.at[p], rows_in, 3, [(0, 4, 1), (4, 4, 1), (12, 4, 1), (8, 4, 1)])
+    to_rows(lambda p: rows_out.at[p], rows_in, 3, [(0, 4, 1), (4, 12, 1)])
     rows_in[me] = rows_out[me]
 
-    wait_all(parts, L - 1, recv_sem.at[2])
-
-    @pl.loop(0, L)
-    def _(p):
-        user_part[pl.ds(p, 1), :] = parts[p]
-
-    user_all[col] = user_part[...].astype(BF16)
+    wait_all(parts, Z - 1, recv_sem.at[2])
+    for z in range(Z):
+        user_part[z : z + 1, :] = parts[z]
+    user_plane[row] = user_part[...].astype(BF16)
+    for d in range(1, 4):
+        pltpu.make_async_remote_copy(
+            user_plane.at[row],
+            user_plane.at[row],
+            send_sem.at[9],
+            recv_sem.at[9],
+            device_id=(over_y(d), col),
+            device_id_type=MESH,
+        ).start()
+
+    wait_all(history, X - 1, recv_sem.at[1])
+
+    @pl.loop(0, X)
+    def _(x):
+        to_core(history.at[2 * x + core], history.at[2 * x + core], 5).start()
+
+    wait_all(user_plane, 4 - 1, recv_sem.at[9])
+    user_all[col] = user_plane[...].reshape(L, 256)
 
     @pl.loop(1, U)
     def _(d):
@@ -251,12 +286,6 @@
             device_id_type=MESH,
         ).start()
 
-    wait_all(history, X - 1, recv_sem.at[1])
-
-    @pl.loop(0, X)
-    def _(x):
-        to_core(history.at[2 * x + core], history.at[2 * x + core], 5).start()
-
     for copy in get_rest:
         copy.wait()
     wait_all(history, X, recv_sem.at[5])
@@ -273,12 +302,15 @@
             user_all[2 * u + 1], items[:, 256:512]
         )
         found = found * D ** (-0.5)
-        for g in range(G):
-            stage[pl.ds(u * G + g, L, stride=ROWS), :] = found[:, g * 128 : (g + 1) * 128]
+        for y in range(4):
+            for g in range(G):
+                stage[pl.ds(y * ROWS + u * G + g, Z, stride=4 * ROWS), :] = found[
+                    y * Z : (y + 1) * Z, g * 128 : (g + 1) * 128
+                ]
     scores_out[...] = stage[...].reshape(L, ROWS, 128).astype(BF16)
     keep = local(scores_out.at[me], scores_in.at[me], 8)
     keep.start()
-    to_rows(lambda p: scores_out.at[p], scores_in, 6, None)
+    to_rows(lambda p: scores_out.at[p], scores_in, 6, [(0, 16, 0)])
 
     wait_all(rows_in, L - 1, recv_sem.at[3])
     stage[...] = rows_in[...].astype(F32).reshape(L * ROWS, 128)
@@ -323,7 +355,8 @@
 
     wait_all(asked, L - 1, send_sem.at[0])
     wait_all(history, X - 1, send_sem.at[1])
-    wait_all(parts, L - 1, send_sem.at[2])
+    wait_all(parts, Z - 1, send_sem.at[2])
+    wait_all(user_plane, 4 - 1, send_sem.at[9])
     wait_all(rows_in, L - 1, send_sem.at[3])
     wait_all(user_all, U - 1, send_sem.at[4])
     wait_all(history, X, send_sem.at[5])
@@ -390,8 +423,9 @@
             pltpu.VMEM((L, 1, 128), F32),
             pltpu.VMEM((L, 1, 128), F32),
             pltpu.VMEM((1, 1, 256), F32),
-            pltpu.VMEM((L, 1, 256), F32),
-            pltpu.VMEM((L, 256), F32),
+            pltpu.VMEM((Z, 1, 256), F32),
+            pltpu.VMEM((Z, 256), F32),
+            pltpu.VMEM((4, Z, 256), BF16),
             pltpu.VMEM((U, L, 256), BF16),
             pltpu.VMEM((L * ROWS, 128), F32),
             pltpu.VMEM((L, ROWS, 128), BF16),
@@ -402,8 +436,9 @@
             pltpu.VMEM((2 * X, OWN, D), BF16),
             pltpu.VMEM((4 * L, D), BF16),
             pltpu.SemaphoreType.DMA((9,)),
-            pltpu.SemaphoreType.DMA((9,)),
-            pltpu.SemaphoreType.DMA((9,)),
+            pltpu.SemaphoreType.DMA((10,)),
+            pltpu.SemaphoreType.DMA((10,)),
+            pltpu.SemaphoreType.REGULAR,
         ],
         compiler_params=pltpu.CompilerParams(
             collective_id=0, has_side_effects=True, vmem_limit_bytes=56 * 2**20

time: 55.9 us -> 54.7 us (0.979)
  Pallas kernels: 54.4 us -> 53.3 us
    pallas_call x1, Pallas kernels: 52.4 us -> 51.3 us  [shards(): pl.pallas_call(kernel, out_shape=(jax.ShapeDtypeStruct((L, ROWS, 128), BF...]
where the time goes in v3:
time: 54.7 us; the launch traced here: 54.6 us
  Pallas kernels  53.3 us (97%)
  between operations  1.29 us (2%)
    pallas_call x1, Pallas kernels, shards(): pl.pallas_call(kernel, out_shape=(jax.ShapeDtypeStruct((L, ROWS, 128), BF...  51.3 us
    pallas_call x1, Pallas kernels, shards(): pl.pallas_call(finish, out_shape=(jax.ShapeDtypeStruct((USERS, PROBES, IT...  1.98 us

profile of v3, /device:TPU:1, one launch (start us, length us, event | category | flops | bytes accessed | tf_op | source)
XLA Modules:
  0.0 54.6 jit_solution(16149450589516695203)
XLA Ops:
  1.3 51.3 %shard_map.104 = (bf16[64,16,128]{2,1,0:T(8,128)(2,1)}, bf16[64,512]{1,0:T(8,128)(2,1)}) custom-call(s32[1,512]{1,0:T(1,128)} %ids_hbm.1, s32[1]{0:T(128)S(6)} %copy.11.length_hbm, bf16[4,512]{1,0:T(4,128)(2,1)} %users_hbm.1, bf16[512,512]{1,0:T(8,128)(2,1)} %bitcast.3, bf16[128,512]{1,0:T(8,128)(2,1)} %bitcast.4, bf16[512,512]{1,0:T(8,128)(2,1)} %wq_hbm.1, ...), custom_call_target="tpu_custom_call" | custom-call | flops 2000000000 | bytes 4000000 | tf_op jit(solution)/shard_map/pallas_call | solution.py:403
  52.6 2.0 %shard_map.105 = (bf16[4,32,512]{2,1,0:T(8,128)(2,1)}, bf16[64,512]{1,0:T(8,128)(2,1)}) custom-call(s32[4,32]{1,0:T(4,128)} %probes_hbm.1, bf16[64,16,128]{2,1,0:T(8,128)(2,1)} %get-tuple-element.6.scores_hbm, bf16[64,512]{1,0:T(8,128)(2,1)} %get-tuple-element.7.ranked_hbm), custom_call_target="tpu_custom_call" | custom-call | flops 20000000 | bytes 1000000 | tf_op jit(solution)/shard_map/pallas_call | solution.py:459

commit v4 on v3

--- a/solution.py
+++ b/solution.py
@@ -145,9 +145,8 @@
         line = jnp.where(lane == k, jnp.sum(slots[k] * place, axis=1, keepdims=True), line)
     request[...] = line
 
-    @pl.loop(0, L)
-    def _(p):
-        ask[p] = request[pl.ds(p, 1), :]
+    for p in range(L):
+        ask[p] = request[p : p + 1, :]
 
     get_users.wait()
     vectors = users[...].astype(F32)
@@ -174,7 +173,7 @@
 
             @pl.loop(1, L)
             def _(d):
-                send(lax.rem(me + d, L))
+                send(jnp.bitwise_and(me + d, L - 1))
 
         else:
             for first, count, rotate in order:
@@ -214,7 +213,7 @@
         some = target.at[pl.ds(0, count)]
         pltpu.make_async_copy(some, some, sem).wait()
 
-    to_rows(lambda p: ask.at[p], asked, 0, None)
+    to_rows(lambda p: ask.at[p], asked, 0, [(8, 8, 1), (0, 8, 1)])
     to_chips(lambda there: history.at[col], lambda d: history.at[col], 1)
     for d in range(1, Z):
         pltpu.make_async_remote_copy(
@@ -238,18 +237,18 @@
     get_items.wait()
     wait_all(asked, L - 1, recv_sem.at[0])
 
-    @pl.loop(0, L)
-    def _(p):
-        request[pl.ds(p, 1), :] = asked[p]
-
+    for p in range(L):
+        request[p : p + 1, :] = asked[p]
     asks = request[...]
     for k in range(SLOTS):
         hot = jnp.where(asks[:, k : k + 1] == iota((L, ITEMS), 1).astype(F32), 1.0, 0.0)
         found = dot(hot.astype(BF16), items[...])
         for g in range(G):
             stage[pl.ds(k * G + g, L, stride=ROWS), :] = found[:, g * 128 : (g + 1) * 128]
-    rows_out[...] = stage[...].reshape(L, ROWS, 128).astype(BF16)
-    to_rows(lambda p: rows_out.at[p], rows_in, 3, [(0, 4, 1), (4, 12, 1)])
+    for first, last in ((0, 16), (16, L)):
+        part_of = stage[first * ROWS : last * ROWS, :]
+        rows_out[first:last] = part_of.reshape(last - first, ROWS, 128).astype(BF16)
+        to_rows(lambda p: rows_out.at[p], rows_in, 3, [(first // 4, (last - first) // 4, 1)])
     rows_in[me] = rows_out[me]
 
     wait_all(parts, Z - 1, recv_sem.at[2])

time: 54.7 us -> 54 us (0.987)
  Pallas kernels: 53.3 us -> 52.3 us
    pallas_call x1, Pallas kernels: 51.3 us -> 50.3 us  [shards(): pl.pallas_call(kernel, out_shape=(jax.ShapeDtypeStruct((L, ROWS, 128), BF...]
where the time goes in v4:
time: 54 us; the launch traced here: 53.6 us
  Pallas kernels  52.3 us (97%)
  between operations  1.29 us (2%)
    pallas_call x1, Pallas kernels, shards(): pl.pallas_call(kernel, out_shape=(jax.ShapeDtypeStruct((L, ROWS, 128), BF...  50.3 us
    pallas_call x1, Pallas kernels, shards(): pl.pallas_call(finish, out_shape=(jax.ShapeDtypeStruct((USERS, PROBES, IT...  1.98 us

profile of v4, /device:TPU:1, one launch (start us, length us, event | category | flops | bytes accessed | tf_op | source)
XLA Modules:
  0.0 53.6 jit_solution(16078097295365847691)
XLA Ops:
  1.3 50.3 %shard_map.104 = (bf16[64,16,128]{2,1,0:T(8,128)(2,1)}, bf16[64,512]{1,0:T(8,128)(2,1)}) custom-call(s32[1,512]{1,0:T(1,128)} %ids_hbm.1, s32[1]{0:T(128)S(6)} %copy.11.length_hbm, bf16[4,512]{1,0:T(4,128)(2,1)} %users_hbm.1, bf16[512,512]{1,0:T(8,128)(2,1)} %bitcast.3, bf16[128,512]{1,0:T(8,128)(2,1)} %bitcast.4, bf16[512,512]{1,0:T(8,128)(2,1)} %wq_hbm.1, ...), custom_call_target="tpu_custom_call" | custom-call | flops 2000000000 | bytes 4000000 | tf_op jit(solution)/shard_map/pallas_call | solution.py:402
  51.6 2.0 %shard_map.105 = (bf16[4,32,512]{2,1,0:T(8,128)(2,1)}, bf16[64,512]{1,0:T(8,128)(2,1)}) custom-call(s32[4,32]{1,0:T(4,128)} %probes_hbm.1, bf16[64,16,128]{2,1,0:T(8,128)(2,1)} %get-tuple-element.6.scores_hbm, bf16[64,512]{1,0:T(8,128)(2,1)} %get-tuple-element.7.ranked_hbm), custom_call_target="tpu_custom_call" | custom-call | flops 20000000 | bytes 1000000 | tf_op jit(solution)/shard_map/pallas_call | solution.py:458

commit v5 on v4

--- a/solution.py
+++ b/solution.py
@@ -245,7 +245,7 @@
         found = dot(hot.astype(BF16), items[...])
         for g in range(G):
             stage[pl.ds(k * G + g, L, stride=ROWS), :] = found[:, g * 128 : (g + 1) * 128]
-    for first, last in ((0, 16), (16, L)):
+    for first, last in ((0, 8), (8, 24), (24, L)):
         part_of = stage[first * ROWS : last * ROWS, :]
         rows_out[first:last] = part_of.reshape(last - first, ROWS, 128).astype(BF16)
         to_rows(lambda p: rows_out.at[p], rows_in, 3, [(first // 4, (last - first) // 4, 1)])

time: 54 us -> 54 us (level)
  the two profiles are of different devices: /device:TPU:1 before, /device:TPU:160 now
where the time goes in v5:
time: 54 us; the launch traced here: 53.8 us
  Pallas kernels  52.5 us (97%)
  between operations  1.29 us (2%)
    pallas_call x1, Pallas kernels, shards(): pl.pallas_call(kernel, out_shape=(jax.ShapeDtypeStruct((L, ROWS, 128), BF...  50.5 us
    pallas_call x1, Pallas kernels, shards(): pl.pallas_call(finish, out_shape=(jax.ShapeDtypeStruct((USERS, PROBES, IT...  1.98 us

profile of v5, /device:TPU:160, one launch (start us, length us, event | category | flops | bytes accessed | tf_op | source)
XLA Modules:
  0.0 53.8 jit_solution(7728047951200535493)
XLA Ops:
  1.3 50.5 %shard_map.104 = (bf16[64,16,128]{2,1,0:T(8,128)(2,1)}, bf16[64,512]{1,0:T(8,128)(2,1)}) custom-call(s32[1,512]{1,0:T(1,128)} %ids_hbm.1, s32[1]{0:T(128)S(6)} %copy.11.length_hbm, bf16[4,512]{1,0:T(4,128)(2,1)} %users_hbm.1, bf16[512,512]{1,0:T(8,128)(2,1)} %bitcast.3, bf16[128,512]{1,0:T(8,128)(2,1)} %bitcast.4, bf16[512,512]{1,0:T(8,128)(2,1)} %wq_hbm.1, ...), custom_call_target="tpu_custom_call" | custom-call | flops 2000000000 | bytes 4000000 | tf_op jit(solution)/shard_map/pallas_call | solution.py:402
  51.8 2.0 %shard_map.105 = (bf16[4,32,512]{2,1,0:T(8,128)(2,1)}, bf16[64,512]{1,0:T(8,128)(2,1)}) custom-call(s32[4,32]{1,0:T(4,128)} %probes_hbm.1, bf16[64,16,128]{2,1,0:T(8,128)(2,1)} %get-tuple-element.6.scores_hbm, bf16[64,512]{1,0:T(8,128)(2,1)} %get-tuple-element.7.ranked_hbm), custom_call_target="tpu_custom_call" | custom-call | flops 20000000 | bytes 1000000 | tf_op jit(solution)/shard_map/pallas_call | solution.py:458
